TPU v7x, 32 devices: a whole 2x2x4 slice. The times are simulated.
32 devices in a mesh: shot: 2 (over x), chan: 16 (over z, y, core).
Axes of the slice: x: 2, y: 2, z: 4, core: 2. Of those that a mesh axis runs over, the one named last changes fastest.
Arguments:
- traces: float32 [8, 256, 4096], P('shot', 'chan'), may hold values from -6 to 6
- shifts: int32 [8, 256], P('shot', 'chan'), may hold values from 0 to 1023
- aperture_lo: int32 [256], P('chan'), may hold values from 0 to 3
- aperture_hi: int32 [256], P('chan'), may hold values from 5 to 8
- dip_band: int32 [256], P('chan'), may hold values from 64 to 512
Outputs:
- filtered: float32 [8, 256, 4096], P(None, ('chan', 'shot'))
All inputs are finite; a program needn't handle non-finite values.
Results may differ from a plain program's by a relative error of at most 0.0003.
Values sent between devices are 32-bit elements; how exact they have to be, the bound alone decides.
A program may use at most 64 MiB of HBM per device.

v0:
```python
import functools
import math

import jax
import jax.numpy as jnp
import numpy as np
from jax import lax
from jax.experimental import pallas as pl
from jax.experimental.pallas import tpu as pltpu
from jax.sharding import PartitionSpec as P

LANES = 128
REACH = 5
HALO = 2 * REACH


def sort_two(a, b):
    return jnp.minimum(a, b), jnp.maximum(a, b)


def median_rows(rows, centers):
    pairs = {}
    fours = {}
    results = {}

    def pair(at):
        if at not in pairs:
            pairs[at] = sort_two(rows[at], rows[at + 1])
        return pairs[at]

    def four(at):
        if at not in fours:
            a, b = pair(at)
            c, d = pair(at + 2)
            low, mid_a = sort_two(a, c)
            mid_b, high = sort_two(b, d)
            mid_a, mid_b = sort_two(mid_a, mid_b)
            fours[at] = (low, mid_a, mid_b, high)
        return fours[at]

    def middle_two(core, extra):
        a, b, c, d = core
        p, q = extra
        low = jnp.minimum(c, jnp.minimum(jnp.maximum(b, p), jnp.maximum(a, q)))
        high = jnp.maximum(b, jnp.maximum(jnp.minimum(d, p), jnp.minimum(c, q)))
        return low, high

    def clamp(value, ends):
        return jnp.maximum(ends[0], jnp.minimum(value, ends[1]))

    last = centers[-1]
    for c in centers[::4]:
        x, y = four(c - 2), four(c + 2)
        low = [jnp.minimum(x[i], y[3 - i]) for i in range(4)]
        high = [jnp.maximum(x[i], y[3 - i]) for i in range(4)]
        core = sort_two(jnp.maximum(low[0], low[2]), jnp.maximum(low[1], low[3])) + sort_two(
            jnp.minimum(high[0], high[2]), jnp.minimum(high[1], high[3])
        )
        ends = middle_two(core, pair(c - 4))
        results[c] = clamp(rows[c - 5], ends)
        results[c + 1] = clamp(rows[c + 6], ends)
        if c + 2 <= last:
            ends = middle_two(core, pair(c + 6))
            results[c + 2] = clamp(rows[c - 3], ends)
            results[c + 3] = clamp(rows[c + 8], ends)
    return results


def turn(value, angle_index, size, sign):
    re, im = value
    angle_index = angle_index % size
    if angle_index == 0:
        return value
    if 4 * angle_index == size:
        return (-im, re) if sign > 0 else (im, -re)
    if 2 * angle_index == size:
        return (-re, -im)
    angle = 2.0 * math.pi * angle_index / size
    cos, sin = math.cos(angle), sign * math.sin(angle)
    if 8 * angle_index == size:
        return ((re - im) * cos, (re + im) * cos) if sign > 0 else ((re + im) * cos, (im - re) * cos)
    return (re * cos - im * sin, re * sin + im * cos)


def add(a, b):
    return (a[0] + b[0], a[1] + b[1])


def sub(a, b):
    return (a[0] - b[0], a[1] - b[1])


def conj(a):
    return (a[0], -a[1])


def complex_dft(values, sign):
    size = len(values)
    if size == 1:
        return values
    even = complex_dft(values[0::2], sign)
    odd = complex_dft(values[1::2], sign)
    odd = [turn(odd[k], k, size, sign) for k in range(size // 2)]
    return [add(even[k], odd[k]) for k in range(size // 2)] + [
        sub(even[k], odd[k]) for k in range(size // 2)
    ]


def real_dft(values):
    size = len(values)
    if size == 2:
        zero = jnp.zeros_like(values[0])
        return [(values[0] + values[1], zero), (values[0] - values[1], zero)]
    even, odd = real_dft(values[0::2]), real_dft(values[1::2])
    half = size // 2
    zero = jnp.zeros_like(values[0])
    result = [None] * (half + 1)
    result[0] = (even[0][0] + odd[0][0], zero)
    result[half] = (even[0][0] - odd[0][0], zero)
    for k in range(1, half // 2 + 1):
        if 2 * k == half:
            result[k] = (even[k][0], -odd[k][0])
        else:
            moved = turn(odd[k], k, size, -1)
            result[k] = add(even[k], moved)
            result[half - k] = conj(sub(even[k], moved))
    return result


def real_inverse(values, size):
    half = size // 2
    if size == 2:
        a, b = values[0][0], values[1][0]
        return [a + b, a - b]
    even, odd = [], []
    for k in range(half // 2 + 1):
        if k == 0:
            even.append((values[0][0] + values[half][0], None))
            odd.append((values[0][0] - values[half][0], None))
        elif 2 * k == half:
            even.append((2.0 * values[k][0], None))
            odd.append((-2.0 * values[k][1], None))
        else:
            other = conj(values[half - k])
            even.append(add(values[k], other))
            odd.append(turn(sub(values[k], other), k, size, 1))
    first, second = real_inverse(even, half), real_inverse(odd, half)
    return [item for both in zip(first, second) for item in both]


def split_dot(x, high_table, low_table):
    high = x.astype(jnp.bfloat16)
    low = (x - high.astype(jnp.float32)).astype(jnp.bfloat16)

    def dot(a, b):
        return jnp.dot(a, b, preferred_element_type=jnp.float32)

    return dot(high, high_table) + (dot(low, high_table) + dot(high, low_table))


def to_sublanes(row, count, start):
    size = row.shape[1]
    row_ids = lax.broadcasted_iota(jnp.int32, (count, size), 0)
    col_ids = lax.broadcasted_iota(jnp.int32, (count, size), 1)
    spread = jnp.broadcast_to(row.astype(jnp.float32), (count, size))
    picked = jnp.where(col_ids == row_ids + start, spread, 0.0)
    return jnp.sum(picked, axis=1, keepdims=True).astype(jnp.int32)


def kernel(
    groups, blocks,
    traces, shifts, lo_ref, hi_ref, band_ref, fwd_hi, fwd_lo, inv_hi, inv_lo, twist,
    out,
    ext, second, up, got, spec,
    halo_send, halo_recv, part_send, part_recv,
):
    shot_local, chan_local, length = traces.shape
    outer = length // LANES
    half = outer // 2 + 1
    rec = chan_local // groups
    shots = groups * shot_local
    ext_rows = (chan_local + 2 * HALO) * outer
    halo_rows = HALO * outer
    part = lax.axis_index("shot")
    block = lax.axis_index("chan")
    mesh_id = pl.DeviceIdType.MESH
    has_left = block > 0
    has_right = block < blocks - 1
    left = jnp.maximum(block - 1, 0)
    right = jnp.minimum(block + 1, blocks - 1)
    q_bits = max((length // 4 // LANES - 1).bit_length(), 0)

    barrier = pltpu.get_barrier_semaphore()

    @pl.when(has_left)
    def _():
        pl.semaphore_signal(barrier, inc=1, device_id=(part, left), device_id_type=mesh_id)

    @pl.when(has_right)
    def _():
        pl.semaphore_signal(barrier, inc=1, device_id=(part, right), device_id_type=mesh_id)

    for offset in range(1, groups):
        pl.semaphore_signal(
            barrier, inc=1, device_id=(lax.rem(part + offset, groups), block), device_id_type=mesh_id
        )

    def rotate_index(column, sign, rows):
        lanes = lax.broadcasted_iota(jnp.int32, (rows, LANES), 1)
        low = jnp.broadcast_to(column & (LANES - 1), (rows, LANES))
        if sign > 0:
            place = lanes + low
            return place & (LANES - 1), place >= LANES
        place = lanes - low
        return place & (LANES - 1), place < 0

    def move(chunks, column, sign, rows):
        index, crossed = rotate_index(column, sign, rows)
        zero = jnp.zeros((rows, LANES), jnp.float32)
        turned = [jnp.take_along_axis(chunk, index, axis=1) for chunk in chunks]

        def at(items, place):
            return items[place] if 0 <= place < outer else zero

        moved = [jnp.where(crossed, at(turned, a + sign), turned[a]) for a in range(outer)]
        for bit in range(q_bits):
            chosen = jnp.broadcast_to((column >> (7 + bit)) & 1, (rows, LANES)) == 1
            stride = sign << bit if sign > 0 else -(1 << bit)
            moved = [jnp.where(chosen, at(moved, a + stride), moved[a]) for a in range(outer)]
        return moved

    def halo_copies(s):
        base = pl.multiple_of(s * ext_rows, 8)
        to_right = pltpu.make_async_remote_copy(
            src_ref=ext.at[pl.ds(base + chan_local * outer, halo_rows)],
            dst_ref=ext.at[pl.ds(base, halo_rows)],
            send_sem=halo_send.at[s, 0],
            recv_sem=halo_recv.at[s, 0],
            device_id=(part, right),
            device_id_type=mesh_id,
        )
        to_left = pltpu.make_async_remote_copy(
            src_ref=ext.at[pl.ds(base + halo_rows, halo_rows)],
            dst_ref=ext.at[pl.ds(base + halo_rows + chan_local * outer, halo_rows)],
            send_sem=halo_send.at[s, 1],
            recv_sem=halo_recv.at[s, 1],
            device_id=(part, left),
            device_id_type=mesh_id,
        )
        return to_right, to_left

    def part_copy(s, offset):
        other = lax.rem(part + offset, groups)
        return pltpu.make_async_remote_copy(
            src_ref=up.at[s, other],
            dst_ref=got.at[part * shot_local + s],
            send_sem=part_send.at[s, offset - 1],
            recv_sem=part_recv.at[s, offset - 1],
            device_id=(other, block),
            device_id_type=mesh_id,
        )

    def align(s):
        row = shifts[pl.ds(s, 1), :]
        for top in range(0, chan_local, 8):
            column = to_sublanes(row, 8, top)
            chunks = [traces[s, top : top + 8, a * LANES : (a + 1) * LANES] for a in range(outer)]
            moved = move(chunks, column, 1, 8)
            for a in range(outer):
                start = s * ext_rows + (HALO + top) * outer + a
                ext[pl.ds(start, 8, stride=outer), :] = moved[a]

    def send_halos(s):
        to_right, to_left = halo_copies(s)

        @pl.when(has_right)
        def _():
            to_right.start()

        @pl.when(has_left)
        def _():
            to_left.start()

    align(0)
    expected = has_left.astype(jnp.int32) + has_right.astype(jnp.int32) + (groups - 1)
    pl.semaphore_wait(barrier, expected)
    send_halos(0)

    def align_step(s, carry):
        align(s)
        send_halos(s)
        return carry

    lax.fori_loop(1, shot_local, align_step, 0)

    @pl.when(jnp.logical_not(has_left))
    def _():
        for s in range(shot_local):
            ext[s * ext_rows : s * ext_rows + halo_rows, :] = jnp.zeros((halo_rows, LANES), jnp.float32)

    @pl.when(jnp.logical_not(has_right))
    def _():
        for s in range(shot_local):
            ext[(s + 1) * ext_rows - halo_rows : (s + 1) * ext_rows, :] = jnp.zeros(
                (halo_rows, LANES), jnp.float32
            )

    def forward(load, shot_id):
        values = real_dft([load(a) for a in range(outer)])
        for c in range(half):
            re, im = values[c]
            cos, sin = twist[0, c : c + 1, :], twist[1, c : c + 1, :]
            spec[shot_id, c, :, 0:LANES] = re * cos + im * sin
            spec[shot_id, c, :, LANES : 2 * LANES] = im * cos - re * sin
        padded = spec.shape[1]
        if padded > half:
            spec[shot_id, half:padded] = jnp.zeros((padded - half, rec, 2 * LANES), jnp.float32)
        flat = spec[shot_id].reshape(padded * rec, 2 * LANES)
        flat = split_dot(flat, fwd_hi[...], fwd_lo[...])
        spec[shot_id] = flat.reshape(padded, rec, 2 * LANES)

    edge_low = jnp.broadcast_to(has_left, (8, LANES))
    edge_high = jnp.broadcast_to(has_right, (8, LANES))

    def clean_step(s, carry):
        to_right, to_left = halo_copies(s)

        @pl.when(has_left)
        def _():
            to_right.wait_recv()

        @pl.when(has_right)
        def _():
            to_left.wait_recv()

        base = s * ext_rows

        def median_step(tile, carry):
            def rows_at(j):
                return ext[pl.ds(pl.multiple_of(base + j * outer + tile * 8, 8), 8), :]

            rows = {j: rows_at(j) for j in range(chan_local + 2 * HALO)}
            centers = list(range(REACH, chan_local + 2 * HALO - REACH))
            found = median_rows(rows, centers)
            cleaned = {}
            for j in centers:
                value = rows[j] - found[j]
                if j < HALO:
                    value = jnp.where(edge_low, value, 0.0)
                elif j >= HALO + chan_local:
                    value = jnp.where(edge_high, value, 0.0)
                cleaned[j] = value
            centers = list(range(HALO, HALO + chan_local))
            found = median_rows(cleaned, centers)
            for j in centers:
                start = pl.multiple_of((j - HALO) * outer + tile * 8, 8)
                second[pl.ds(start, 8), :] = cleaned[j] - found[j]
            return carry

        lax.fori_loop(0, outer // 8, median_step, 0)

        shot_id = part * shot_local + s
        row = shifts[pl.ds(s, 1), :]
        for g in range(groups):
            column = to_sublanes(row, rec, g * rec)
            low = to_sublanes(lo_ref[...], rec, g * rec)
            high = to_sublanes(hi_ref[...], rec, g * rec)
            inside = jnp.broadcast_to(((low <= shot_id) & (high > shot_id)).astype(jnp.int32), (rec, LANES)) == 1
            chunks = [
                second[pl.ds(g * rec * outer + a, rec, stride=outer), :] for a in range(outer)
            ]
            moved = move(chunks, column, -1, rec)
            for a in range(outer):
                up[s, g, a] = jnp.where(inside, moved[a], 0.0)
        for offset in range(1, groups):
            part_copy(s, offset).start()
        forward(lambda a: up[s, part, a], shot_id)
        return carry

    lax.fori_loop(0, shot_local, clean_step, 0)

    def arrive_step(s, carry):
        for offset in range(1, groups):
            part_copy(s, offset).wait_recv()
            source = lax.rem(part + groups - offset, groups)
            shot_id = source * shot_local + s
            forward(lambda a: got[shot_id, a], shot_id)
        return carry

    lax.fori_loop(0, shot_local, arrive_step, 0)

    band = jnp.broadcast_to(to_sublanes(band_ref[...], rec, part * rec), (rec, LANES))
    lane_ids = lax.broadcasted_iota(jnp.int32, (rec, LANES), 1)

    def dip_step(c, carry):
        frequency = lane_ids * outer + c
        freq_abs = jnp.minimum(frequency, length - frequency)
        values = [
            (spec[s, c, :, 0:LANES], spec[s, c, :, LANES : 2 * LANES]) for s in range(shots)
        ]
        waves = complex_dft(values, -1)
        kept = []
        for k in range(shots):
            keep = min(k, shots - k) * band <= freq_abs
            kept.append((jnp.where(keep, waves[k][0], 0.0), jnp.where(keep, waves[k][1], 0.0)))
        values = complex_dft(kept, 1)
        for s in range(shots):
            spec[s, c, :, 0:LANES] = values[s][0]
            spec[s, c, :, LANES : 2 * LANES] = values[s][1]
        return carry

    lax.fori_loop(0, half, dip_step, 0)

    def back_step(s, carry):
        padded = spec.shape[1]
        flat = spec[s].reshape(padded * rec, 2 * LANES)
        flat = split_dot(flat, inv_hi[...], inv_lo[...])
        spec[s] = flat.reshape(padded, rec, 2 * LANES)
        values = []
        for c in range(half):
            re, im = spec[s, c, :, 0:LANES], spec[s, c, :, LANES : 2 * LANES]
            cos, sin = twist[0, c : c + 1, :], twist[1, c : c + 1, :]
            values.append((re * cos - im * sin, im * cos + re * sin))
        for a, value in enumerate(real_inverse(values, outer)):
            out[s, :, a * LANES : (a + 1) * LANES] = value
        return carry

    lax.fori_loop(0, shots, back_step, 0)

    def drain_step(s, carry):
        to_right, to_left = halo_copies(s)

        @pl.when(has_right)
        def _():
            to_right.wait_send()

        @pl.when(has_left)
        def _():
            to_left.wait_send()

        for offset in range(1, groups):
            part_copy(s, offset).wait_send()
        return carry

    lax.fori_loop(0, shot_local, drain_step, 0)


def halves(table):
    high = table.astype(jnp.bfloat16)
    return high, (table - high.astype(np.float64)).astype(jnp.bfloat16)


def tables(shots, length):
    outer = length // LANES
    ids = np.arange(LANES)
    angles = 2.0 * np.pi * (np.outer(ids, ids) % LANES) / LANES
    cos, sin = np.cos(angles), np.sin(angles)
    forward = np.block([[cos, -sin], [sin, cos]])
    inverse = np.block([[cos, sin], [-sin, cos]]) / (shots * length)
    product = np.outer(np.arange(outer // 2 + 1), ids) % length
    angles = 2.0 * np.pi * product / length
    twist = np.stack([np.cos(angles), np.sin(angles)]).astype(np.float32)
    return halves(forward) + halves(inverse) + (twist,)


def local(groups, blocks, traces, shifts, aperture_lo, aperture_hi, dip_band):
    shot_local, chan_local, length = traces.shape
    outer = length // LANES
    rec = chan_local // groups
    shots = groups * shot_local
    padded = outer // 2 + 2
    constants = [jnp.asarray(table) for table in tables(shots, length)]
    vmem = pl.BlockSpec(memory_space=pltpu.VMEM)
    others = max(groups - 1, 1)
    return pl.pallas_call(
        functools.partial(kernel, groups, blocks),
        out_shape=jax.ShapeDtypeStruct((shots, rec, length), jnp.float32),
        in_specs=[vmem] * 10,
        out_specs=vmem,
        scratch_shapes=[
            pltpu.VMEM((shot_local * (chan_local + 2 * HALO) * outer, LANES), jnp.float32),
            pltpu.VMEM((chan_local * outer, LANES), jnp.float32),
            pltpu.VMEM((shot_local, groups, outer, rec, LANES), jnp.float32),
            pltpu.VMEM((shots, outer, rec, LANES), jnp.float32),
            pltpu.VMEM((shots, padded, rec, 2 * LANES), jnp.float32),
            pltpu.SemaphoreType.DMA((shot_local, 2)),
            pltpu.SemaphoreType.DMA((shot_local, 2)),
            pltpu.SemaphoreType.DMA((shot_local, others)),
            pltpu.SemaphoreType.DMA((shot_local, others)),
        ],
        compiler_params=pltpu.CompilerParams(
            collective_id=0, has_side_effects=True, vmem_limit_bytes=48 * 1024 * 1024
        ),
    )(
        traces, shifts, aperture_lo[None, :], aperture_hi[None, :], dip_band[None, :], *constants
    )


def solution(mesh):
    return jax.shard_map(
        functools.partial(local, mesh.shape["shot"], mesh.shape["chan"]),
        mesh=mesh,
        in_specs=(P("shot", "chan", None), P("shot", "chan"), P("chan"), P("chan"), P("chan")),
        out_specs=P(None, ("chan", "shot"), None),
        check_vma=False,
    )
```

profile of v0, /device:TPU:9, one launch (start us, length us, event | category | flops | bytes accessed | tf_op | source)
XLA Modules:
  0.0 32.2 jit_solution(5052166295362938437)
XLA Ops:
  0.0 0.0 copy-start.6
  0.0 0.0 copy-start.7
  0.0 0.0 copy-start.8
  0.0 0.0 copy-start.9
  0.0 0.7 %copy-done.6 = s32[4,16]{1,0:T(4,128)S(1)} copy-done((s32[4,16]{1,0:T(4,128)S(1)}, s32[4,16]{1,0:T(4,128)}, u32[]{:S(2)}) %copy-start.6) | copy-done | bytes 280
  0.7 0.0 copy-done.7
  0.7 0.0 copy-done.8
  0.7 0.0 copy-done.9
  0.7 0.0 copy-start
  0.7 1.2 %copy-done = f32[4,16,4096]{2,1,0:T(8,128)S(1)} copy-done((f32[4,16,4096]{2,1,0:T(8,128)S(1)}, f32[4,16,4096]{2,1,0:T(8,128)}, u32[]{:S(2)}) %copy-start) | copy-done | bytes 1048600
  1.9 0.0 copy-start.1
  1.9 0.9 %copy-done.1 = bf16[256,256]{1,0:T(8,128)(2,1)S(1)} copy-done((bf16[256,256]{1,0:T(8,128)(2,1)S(1)}, bf16[256,256]{1,0:T(8,128)(2,1)}, u32[]{:S(2)}) %copy-start.1) | copy-done | bytes 131096
  2.8 0.0 copy-start.2
  2.8 0.9 %copy-done.2 = bf16[256,256]{1,0:T(8,128)(2,1)S(1)} copy-done((bf16[256,256]{1,0:T(8,128)(2,1)S(1)}, bf16[256,256]{1,0:T(8,128)(2,1)}, u32[]{:S(2)}) %copy-start.2) | copy-done | bytes 131096
  3.7 0.0 copy-start.3
  3.7 0.9 %copy-done.3 = bf16[256,256]{1,0:T(8,128)(2,1)S(1)} copy-done((bf16[256,256]{1,0:T(8,128)(2,1)S(1)}, bf16[256,256]{1,0:T(8,128)(2,1)}, u32[]{:S(2)}) %copy-start.3) | copy-done | bytes 131096
  4.6 0.0 copy-start.4
  4.6 0.9 %copy-done.4 = bf16[256,256]{1,0:T(8,128)(2,1)S(1)} copy-done((bf16[256,256]{1,0:T(8,128)(2,1)S(1)}, bf16[256,256]{1,0:T(8,128)(2,1)}, u32[]{:S(2)}) %copy-start.4) | copy-done | bytes 131096
  5.5 0.0 copy-start.5
  5.5 0.7 %copy-done.5 = f32[2,17,128]{2,1,0:T(8,128)S(1)} copy-done((f32[2,17,128]{2,1,0:T(8,128)S(1)}, f32[2,17,128]{2,1,0:T(8,128)}, u32[]{:S(2)}) %copy-start.5) | copy-done | bytes 17432
  6.3 24.9 %shard_map.100 = f32[8,8,4096]{2,1,0:T(8,128)S(1)} custom-call(f32[4,16,4096]{2,1,0:T(8,128)S(1)} %copy-done, s32[4,16]{1,0:T(4,128)S(1)} %copy-done.6, s32[1,16]{1,0:T(1,128)S(1)} %bitcast.3, s32[1,16]{1,0:T(1,128)S(1)} %bitcast.4, s32[1,16]{1,0:T(1,128)S(1)} %bitcast.5, bf16[256,256]{1,0:T(8,128)(2,1)S(1)} %copy-done.4, bf16[256,256]{1,0:T(8,128)(2,1)S(1)} %copy-done.3, ...), custom_call_target="tpu_custom_call" | custom-call | tf_op jit(solution)/shard_map/pallas_call | solution.py:475
  31.2 1.0 %copy.12 = f32[8,8,4096]{2,1,0:T(8,128)} copy(f32[8,8,4096]{2,1,0:T(8,128)S(1)} %shard_map.100) | data formatting | bytes 2097152
Async XLA Ops:
  0.0 0.7 %copy-start.6 = (s32[4,16]{1,0:T(4,128)S(1)}, s32[4,16]{1,0:T(4,128)}, u32[]{:S(2)}) copy-start(s32[4,16]{1,0:T(4,128)} %shifts.1) | copy-start | bytes 772
  0.0 0.7 %copy-start.7 = (s32[16]{0:T(128)S(1)}, s32[16]{0:T(128)}, u32[]{:S(2)}) copy-start(s32[16]{0:T(128)} %param.12) | copy-start | bytes 196
  0.0 0.7 %copy-start.8 = (s32[16]{0:T(128)S(1)}, s32[16]{0:T(128)}, u32[]{:S(2)}) copy-start(s32[16]{0:T(128)} %param.13) | copy-start | bytes 196
  0.0 0.7 %copy-start.9 = (s32[16]{0:T(128)S(1)}, s32[16]{0:T(128)}, u32[]{:S(2)}) copy-start(s32[16]{0:T(128)} %param.14) | copy-start | bytes 196
  0.7 1.2 %copy-start = (f32[4,16,4096]{2,1,0:T(8,128)S(1)}, f32[4,16,4096]{2,1,0:T(8,128)}, u32[]{:S(2)}) copy-start(f32[4,16,4096]{2,1,0:T(8,128)} %traces.1) | copy-start | bytes 3145732
  1.9 0.9 %copy-start.1 = (bf16[256,256]{1,0:T(8,128)(2,1)S(1)}, bf16[256,256]{1,0:T(8,128)(2,1)}, u32[]{:S(2)}) copy-start(bf16[256,256]{1,0:T(8,128)(2,1)} %constant.13.clone.inv_lo) | copy-start | bytes 393220
  2.8 0.9 %copy-start.2 = (bf16[256,256]{1,0:T(8,128)(2,1)S(1)}, bf16[256,256]{1,0:T(8,128)(2,1)}, u32[]{:S(2)}) copy-start(bf16[256,256]{1,0:T(8,128)(2,1)} %constant.12.clone.inv_hi) | copy-start | bytes 393220
  3.7 0.9 %copy-start.3 = (bf16[256,256]{1,0:T(8,128)(2,1)S(1)}, bf16[256,256]{1,0:T(8,128)(2,1)}, u32[]{:S(2)}) copy-start(bf16[256,256]{1,0:T(8,128)(2,1)} %constant.11.clone.fwd_lo) | copy-start | bytes 393220
  4.6 0.9 %copy-start.4 = (bf16[256,256]{1,0:T(8,128)(2,1)S(1)}, bf16[256,256]{1,0:T(8,128)(2,1)}, u32[]{:S(2)}) copy-start(bf16[256,256]{1,0:T(8,128)(2,1)} %constant.10.clone.fwd_hi) | copy-start | bytes 393220
  5.5 0.7 %copy-start.5 = (f32[2,17,128]{2,1,0:T(8,128)S(1)}, f32[2,17,128]{2,1,0:T(8,128)}, u32[]{:S(2)}) copy-start(f32[2,17,128]{2,1,0:T(8,128)} %constant.14.clone.twist) | copy-start | bytes 52228
where the time goes:
time: 32.8 us; the launch traced here: 32.2 us
  Pallas kernels  24.9 us (76%)
  local copies, waits for them, and re-layouts  7.24 us (22%)
    pallas_call x1, Pallas kernels, local(): pl.pallas_call(functools.partial(kernel, groups, blocks), out_shape=jax.S...  24.9 us
    unnamed x21, local copies, waits for them, and re-layouts  7.24 us

commit v1 on v0

--- a/solution.py
+++ b/solution.py
@@ -169,11 +169,12 @@
 
 def kernel(
     groups, blocks,
-    traces, shifts, lo_ref, hi_ref, band_ref, fwd_hi, fwd_lo, inv_hi, inv_lo, twist,
-    out,
-    ext, second, up, got, spec,
-    halo_send, halo_recv, part_send, part_recv,
+    traces_hbm, *rest,
 ):
+    small_hbm, (out,), scratch = rest[:9], rest[9:10], rest[10:]
+    traces, small, scratch = scratch[0], scratch[1:10], scratch[10:]
+    shifts, lo_ref, hi_ref, band_ref, fwd_hi, fwd_lo, inv_hi, inv_lo, twist = small
+    ext, second, up, got, spec, halo_send, halo_recv, part_send, part_recv, load_sem, small_sem = scratch
     shot_local, chan_local, length = traces.shape
     outer = length // LANES
     half = outer // 2 + 1
@@ -189,6 +190,16 @@
     left = jnp.maximum(block - 1, 0)
     right = jnp.minimum(block + 1, blocks - 1)
     q_bits = max((length // 4 // LANES - 1).bit_length(), 0)
+
+    small_loads = [
+        pltpu.make_async_copy(small_hbm[i], small[i], small_sem.at[i]) for i in range(len(small))
+    ]
+    trace_loads = [
+        pltpu.make_async_copy(traces_hbm.at[s], traces.at[s], load_sem.at[s]) for s in range(shot_local)
+    ]
+    small_loads[0].start()
+    for load in trace_loads + small_loads[1:]:
+        load.start()
 
     barrier = pltpu.get_barrier_semaphore()
 
@@ -281,6 +292,8 @@
         def _():
             to_left.start()
 
+    small_loads[0].wait()
+    trace_loads[0].wait()
     align(0)
     expected = has_left.astype(jnp.int32) + has_right.astype(jnp.int32) + (groups - 1)
     pl.semaphore_wait(barrier, expected)
@@ -291,7 +304,11 @@
         send_halos(s)
         return carry
 
+    for load in trace_loads[1:]:
+        load.wait()
     lax.fori_loop(1, shot_local, align_step, 0)
+    for load in small_loads[1:]:
+        load.wait()
 
     @pl.when(jnp.logical_not(has_left))
     def _():
@@ -375,19 +392,22 @@
         for offset in range(1, groups):
             part_copy(s, offset).start()
         forward(lambda a: up[s, part, a], shot_id)
+
+        @pl.when(s > 0)
+        def _():
+            arrive(s - 1)
+
         return carry
 
-    lax.fori_loop(0, shot_local, clean_step, 0)
-
-    def arrive_step(s, carry):
+    def arrive(s):
         for offset in range(1, groups):
             part_copy(s, offset).wait_recv()
             source = lax.rem(part + groups - offset, groups)
             shot_id = source * shot_local + s
             forward(lambda a: got[shot_id, a], shot_id)
-        return carry
-
-    lax.fori_loop(0, shot_local, arrive_step, 0)
+
+    lax.fori_loop(0, shot_local, clean_step, 0)
+    arrive(shot_local - 1)
 
     band = jnp.broadcast_to(to_sublanes(band_ref[...], rec, part * rec), (rec, LANES))
     lane_ids = lax.broadcasted_iota(jnp.int32, (rec, LANES), 1)
@@ -411,11 +431,14 @@
 
     lax.fori_loop(0, half, dip_step, 0)
 
+    padded = spec.shape[1]
+    batch = shots // 2
+    for first in range(0, shots, batch):
+        flat = spec[first : first + batch].reshape(batch * padded * rec, 2 * LANES)
+        flat = split_dot(flat, inv_hi[...], inv_lo[...])
+        spec[first : first + batch] = flat.reshape(batch, padded, rec, 2 * LANES)
+
     def back_step(s, carry):
-        padded = spec.shape[1]
-        flat = spec[s].reshape(padded * rec, 2 * LANES)
-        flat = split_dot(flat, inv_hi[...], inv_lo[...])
-        spec[s] = flat.reshape(padded, rec, 2 * LANES)
         values = []
         for c in range(half):
             re, im = spec[s, c, :, 0:LANES], spec[s, c, :, LANES : 2 * LANES]
@@ -470,14 +493,16 @@
     shots = groups * shot_local
     padded = outer // 2 + 2
     constants = [jnp.asarray(table) for table in tables(shots, length)]
-    vmem = pl.BlockSpec(memory_space=pltpu.VMEM)
+    operands = [
+        traces, shifts, aperture_lo[None, :], aperture_hi[None, :], dip_band[None, :], *constants
+    ]
     others = max(groups - 1, 1)
     return pl.pallas_call(
         functools.partial(kernel, groups, blocks),
         out_shape=jax.ShapeDtypeStruct((shots, rec, length), jnp.float32),
-        in_specs=[vmem] * 10,
-        out_specs=vmem,
-        scratch_shapes=[
+        in_specs=[pl.BlockSpec(memory_space=pltpu.HBM)] * len(operands),
+        out_specs=pl.BlockSpec(memory_space=pltpu.VMEM),
+        scratch_shapes=[pltpu.VMEM(item.shape, item.dtype) for item in operands] + [
             pltpu.VMEM((shot_local * (chan_local + 2 * HALO) * outer, LANES), jnp.float32),
             pltpu.VMEM((chan_local * outer, LANES), jnp.float32),
             pltpu.VMEM((shot_local, groups, outer, rec, LANES), jnp.float32),
@@ -487,13 +512,13 @@
             pltpu.SemaphoreType.DMA((shot_local, 2)),
             pltpu.SemaphoreType.DMA((shot_local, others)),
             pltpu.SemaphoreType.DMA((shot_local, others)),
+            pltpu.SemaphoreType.DMA((shot_local,)),
+            pltpu.SemaphoreType.DMA((len(operands) - 1,)),
         ],
         compiler_params=pltpu.CompilerParams(
             collective_id=0, has_side_effects=True, vmem_limit_bytes=48 * 1024 * 1024
         ),
-    )(
-        traces, shifts, aperture_lo[None, :], aperture_hi[None, :], dip_band[None, :], *constants
-    )
+    )(*operands)
 
 
 def solution(mesh):

time: 32.8 us -> 34.4 us (1.049)
  Pallas kernels: 24.9 us -> 26.8 us
    pallas_call x1, Pallas kernels: 24.9 us -> 26.8 us  [local(): pl.pallas_call(functools.partial(kernel, groups, blocks), out_shape=jax.S...]
where the time goes in v1:
time: 34.4 us; the launch traced here: 34.1 us
  Pallas kernels  26.8 us (78%)
  local copies, waits for them, and re-layouts  7.24 us (21%)
    pallas_call x1, Pallas kernels, local(): pl.pallas_call(functools.partial(kernel, groups, blocks), out_shape=jax.S...  26.8 us
    unnamed x21, local copies, waits for them, and re-layouts  7.24 us

profile of v1, /device:TPU:9, one launch (start us, length us, event | category | flops | bytes accessed | tf_op | source)
XLA Modules:
  0.0 34.1 jit_solution(10376740437063106844)
XLA Ops:
  0.0 0.0 copy-start.6
  0.0 0.0 copy-start.7
  0.0 0.0 copy-start.8
  0.0 0.0 copy-start.9
  0.0 0.7 %copy-done.6 = s32[4,16]{1,0:T(4,128)S(1)} copy-done((s32[4,16]{1,0:T(4,128)S(1)}, s32[4,16]{1,0:T(4,128)}, u32[]{:S(2)}) %copy-start.6) | copy-done | bytes 280
  0.7 0.0 copy-done.7
  0.7 0.0 copy-done.8
  0.7 0.0 copy-done.9
  0.7 0.0 copy-start
  0.7 1.2 %copy-done = f32[4,16,4096]{2,1,0:T(8,128)S(1)} copy-done((f32[4,16,4096]{2,1,0:T(8,128)S(1)}, f32[4,16,4096]{2,1,0:T(8,128)}, u32[]{:S(2)}) %copy-start) | copy-done | bytes 1048600
  1.9 0.0 copy-start.1
  1.9 0.9 %copy-done.1 = bf16[256,256]{1,0:T(8,128)(2,1)S(1)} copy-done((bf16[256,256]{1,0:T(8,128)(2,1)S(1)}, bf16[256,256]{1,0:T(8,128)(2,1)}, u32[]{:S(2)}) %copy-start.1) | copy-done | bytes 131096
  2.8 0.0 copy-start.2
  2.8 0.9 %copy-done.2 = bf16[256,256]{1,0:T(8,128)(2,1)S(1)} copy-done((bf16[256,256]{1,0:T(8,128)(2,1)S(1)}, bf16[256,256]{1,0:T(8,128)(2,1)}, u32[]{:S(2)}) %copy-start.2) | copy-done | bytes 131096
  3.7 0.0 copy-start.3
  3.7 0.9 %copy-done.3 = bf16[256,256]{1,0:T(8,128)(2,1)S(1)} copy-done((bf16[256,256]{1,0:T(8,128)(2,1)S(1)}, bf16[256,256]{1,0:T(8,128)(2,1)}, u32[]{:S(2)}) %copy-start.3) | copy-done | bytes 131096
  4.6 0.0 copy-start.4
  4.6 0.9 %copy-done.4 = bf16[256,256]{1,0:T(8,128)(2,1)S(1)} copy-done((bf16[256,256]{1,0:T(8,128)(2,1)S(1)}, bf16[256,256]{1,0:T(8,128)(2,1)}, u32[]{:S(2)}) %copy-start.4) | copy-done | bytes 131096
  5.5 0.0 copy-start.5
  5.5 0.7 %copy-done.5 = f32[2,17,128]{2,1,0:T(8,128)S(1)} copy-done((f32[2,17,128]{2,1,0:T(8,128)S(1)}, f32[2,17,128]{2,1,0:T(8,128)}, u32[]{:S(2)}) %copy-start.5) | copy-done | bytes 17432
  6.3 26.8 %shard_map.100 = f32[8,8,4096]{2,1,0:T(8,128)S(1)} custom-call(f32[4,16,4096]{2,1,0:T(8,128)S(1)} %copy-done, s32[4,16]{1,0:T(4,128)S(1)} %copy-done.6, s32[1,16]{1,0:T(1,128)S(1)} %bitcast.3, s32[1,16]{1,0:T(1,128)S(1)} %bitcast.4, s32[1,16]{1,0:T(1,128)S(1)} %bitcast.5, bf16[256,256]{1,0:T(8,128)(2,1)S(1)} %copy-done.4, bf16[256,256]{1,0:T(8,128)(2,1)S(1)} %copy-done.3, ...), custom_call_target="tpu_custom_call" | custom-call | tf_op jit(solution)/shard_map/pallas_call | solution.py:500
  33.1 1.0 %copy.12 = f32[8,8,4096]{2,1,0:T(8,128)} copy(f32[8,8,4096]{2,1,0:T(8,128)S(1)} %shard_map.100) | data formatting | bytes 2097152
Async XLA Ops:
  0.0 0.7 %copy-start.6 = (s32[4,16]{1,0:T(4,128)S(1)}, s32[4,16]{1,0:T(4,128)}, u32[]{:S(2)}) copy-start(s32[4,16]{1,0:T(4,128)} %rest_0_.1) | copy-start | bytes 772
  0.0 0.7 %copy-start.7 = (s32[16]{0:T(128)S(1)}, s32[16]{0:T(128)}, u32[]{:S(2)}) copy-start(s32[16]{0:T(128)} %param.12) | copy-start | bytes 196
  0.0 0.7 %copy-start.8 = (s32[16]{0:T(128)S(1)}, s32[16]{0:T(128)}, u32[]{:S(2)}) copy-start(s32[16]{0:T(128)} %param.13) | copy-start | bytes 196
  0.0 0.7 %copy-start.9 = (s32[16]{0:T(128)S(1)}, s32[16]{0:T(128)}, u32[]{:S(2)}) copy-start(s32[16]{0:T(128)} %param.14) | copy-start | bytes 196
  0.7 1.2 %copy-start = (f32[4,16,4096]{2,1,0:T(8,128)S(1)}, f32[4,16,4096]{2,1,0:T(8,128)}, u32[]{:S(2)}) copy-start(f32[4,16,4096]{2,1,0:T(8,128)} %traces_hbm.1) | copy-start | bytes 3145732
  1.9 0.9 %copy-start.1 = (bf16[256,256]{1,0:T(8,128)(2,1)S(1)}, bf16[256,256]{1,0:T(8,128)(2,1)}, u32[]{:S(2)}) copy-start(bf16[256,256]{1,0:T(8,128)(2,1)} %constant.13.clone.rest_7_) | copy-start | bytes 393220
  2.8 0.9 %copy-start.2 = (bf16[256,256]{1,0:T(8,128)(2,1)S(1)}, bf16[256,256]{1,0:T(8,128)(2,1)}, u32[]{:S(2)}) copy-start(bf16[256,256]{1,0:T(8,128)(2,1)} %constant.12.clone.rest_6_) | copy-start | bytes 393220
  3.7 0.9 %copy-start.3 = (bf16[256,256]{1,0:T(8,128)(2,1)S(1)}, bf16[256,256]{1,0:T(8,128)(2,1)}, u32[]{:S(2)}) copy-start(bf16[256,256]{1,0:T(8,128)(2,1)} %constant.11.clone.rest_5_) | copy-start | bytes 393220
  4.6 0.9 %copy-start.4 = (bf16[256,256]{1,0:T(8,128)(2,1)S(1)}, bf16[256,256]{1,0:T(8,128)(2,1)}, u32[]{:S(2)}) copy-start(bf16[256,256]{1,0:T(8,128)(2,1)} %constant.10.clone.rest_4_) | copy-start | bytes 393220
  5.5 0.7 %copy-start.5 = (f32[2,17,128]{2,1,0:T(8,128)S(1)}, f32[2,17,128]{2,1,0:T(8,128)}, u32[]{:S(2)}) copy-start(f32[2,17,128]{2,1,0:T(8,128)} %constant.14.clone.rest_8_) | copy-start | bytes 52228

commit v2 on v1

--- a/solution.py
+++ b/solution.py
@@ -171,17 +171,21 @@
     groups, blocks,
     traces_hbm, *rest,
 ):
-    small_hbm, (out,), scratch = rest[:9], rest[9:10], rest[10:]
-    traces, small, scratch = scratch[0], scratch[1:10], scratch[10:]
-    shifts, lo_ref, hi_ref, band_ref, fwd_hi, fwd_lo, inv_hi, inv_lo, twist = small
-    ext, second, up, got, spec, halo_send, halo_recv, part_send, part_recv, load_sem, small_sem = scratch
+    small_hbm, out_hbm, scratch = rest[:6], rest[6], rest[7:]
+    traces, small, scratch = scratch[0], scratch[1:7], scratch[7:]
+    shifts, lo_ref, hi_ref, band_ref, table, twist = small
+    ext, second, up, got, spec, out, table_hi, table_lo = scratch[:8]
+    halo_send, halo_recv, part_send, part_recv, load_sem, small_sem, out_sem = scratch[8:]
     shot_local, chan_local, length = traces.shape
     outer = length // LANES
     half = outer // 2 + 1
     rec = chan_local // groups
     shots = groups * shot_local
-    ext_rows = (chan_local + 2 * HALO) * outer
-    halo_rows = HALO * outer
+    tiles = outer // 8
+    back = outer // 4
+    span = outer + back
+    unit_rows = (chan_local + 2 * HALO) * 8
+    halo_rows = HALO * 8
     part = lax.axis_index("shot")
     block = lax.axis_index("chan")
     mesh_id = pl.DeviceIdType.MESH
@@ -225,48 +229,64 @@
         place = lanes - low
         return place & (LANES - 1), place < 0
 
-    def move(chunks, column, sign, rows):
-        index, crossed = rotate_index(column, sign, rows)
+    def whole_chunks(column, rows):
+        return [
+            jnp.broadcast_to((column >> (7 + bit)) & 1, (rows, LANES)) == 1 for bit in range(q_bits)
+        ]
+
+    def move_earlier(chunks, column, rows):
+        index, crossed = rotate_index(column, 1, rows)
         zero = jnp.zeros((rows, LANES), jnp.float32)
         turned = [jnp.take_along_axis(chunk, index, axis=1) for chunk in chunks]
 
         def at(items, place):
-            return items[place] if 0 <= place < outer else zero
-
-        moved = [jnp.where(crossed, at(turned, a + sign), turned[a]) for a in range(outer)]
-        for bit in range(q_bits):
-            chosen = jnp.broadcast_to((column >> (7 + bit)) & 1, (rows, LANES)) == 1
-            stride = sign << bit if sign > 0 else -(1 << bit)
-            moved = [jnp.where(chosen, at(moved, a + stride), moved[a]) for a in range(outer)]
+            return items[place] if place < outer else zero
+
+        moved = [jnp.where(crossed, at(turned, a + 1), turned[a]) for a in range(outer)]
+        for bit, chosen in enumerate(whole_chunks(column, rows)):
+            moved = [jnp.where(chosen, at(moved, a + (1 << bit)), moved[a]) for a in range(outer)]
         return moved
 
-    def halo_copies(s):
-        base = pl.multiple_of(s * ext_rows, 8)
+    def move_later(chunks, chosen, index, crossed):
+        moved = dict(enumerate(chunks))
+        first = back + 8 - len(chunks)
+        for bit in reversed(range(q_bits)):
+            first += 1 << bit
+            moved = {
+                a: jnp.where(chosen[bit], moved[a - (1 << bit)], moved[a])
+                for a in range(first, back + 8)
+            }
+        turned = {a: jnp.take_along_axis(moved[a], index, axis=1) for a in range(back - 1, back + 8)}
+        return [jnp.where(crossed, turned[a - 1], turned[a]) for a in range(back, back + 8)]
+
+    def halo_copies(unit):
+        base = pl.multiple_of(unit * unit_rows, 8)
         to_right = pltpu.make_async_remote_copy(
-            src_ref=ext.at[pl.ds(base + chan_local * outer, halo_rows)],
+            src_ref=ext.at[pl.ds(base + chan_local * 8, halo_rows)],
             dst_ref=ext.at[pl.ds(base, halo_rows)],
-            send_sem=halo_send.at[s, 0],
-            recv_sem=halo_recv.at[s, 0],
+            send_sem=halo_send.at[unit, 0],
+            recv_sem=halo_recv.at[unit, 0],
             device_id=(part, right),
             device_id_type=mesh_id,
         )
         to_left = pltpu.make_async_remote_copy(
             src_ref=ext.at[pl.ds(base + halo_rows, halo_rows)],
-            dst_ref=ext.at[pl.ds(base + halo_rows + chan_local * outer, halo_rows)],
-            send_sem=halo_send.at[s, 1],
-            recv_sem=halo_recv.at[s, 1],
+            dst_ref=ext.at[pl.ds(base + halo_rows + chan_local * 8, halo_rows)],
+            send_sem=halo_send.at[unit, 1],
+            recv_sem=halo_recv.at[unit, 1],
             device_id=(part, left),
             device_id_type=mesh_id,
         )
         return to_right, to_left
 
-    def part_copy(s, offset):
+    def part_copy(s, tile, offset):
         other = lax.rem(part + offset, groups)
+        rows = pl.ds(pl.multiple_of(tile * 8, 8), 8)
         return pltpu.make_async_remote_copy(
-            src_ref=up.at[s, other],
-            dst_ref=got.at[part * shot_local + s],
-            send_sem=part_send.at[s, offset - 1],
-            recv_sem=part_recv.at[s, offset - 1],
+            src_ref=up.at[s, other, rows],
+            dst_ref=got.at[part * shot_local + s, rows],
+            send_sem=part_send.at[s * tiles + tile, offset - 1],
+            recv_sem=part_recv.at[s * tiles + tile, offset - 1],
             device_id=(other, block),
             device_id_type=mesh_id,
         )
@@ -276,21 +296,16 @@
         for top in range(0, chan_local, 8):
             column = to_sublanes(row, 8, top)
             chunks = [traces[s, top : top + 8, a * LANES : (a + 1) * LANES] for a in range(outer)]
-            moved = move(chunks, column, 1, 8)
+            moved = move_earlier(chunks, column, 8)
             for a in range(outer):
-                start = s * ext_rows + (HALO + top) * outer + a
-                ext[pl.ds(start, 8, stride=outer), :] = moved[a]
+                start = (s * tiles + a // 8) * unit_rows + (HALO + top) * 8 + a % 8
+                ext[pl.ds(start, 8, stride=8), :] = moved[a]
 
     def send_halos(s):
-        to_right, to_left = halo_copies(s)
-
-        @pl.when(has_right)
-        def _():
-            to_right.start()
-
-        @pl.when(has_left)
-        def _():
-            to_left.start()
+        for tile in range(tiles):
+            to_right, to_left = halo_copies(s * tiles + tile)
+            pl.when(has_right)(to_right.start)
+            pl.when(has_left)(to_left.start)
 
     small_loads[0].wait()
     trace_loads[0].wait()
@@ -309,18 +324,21 @@
     lax.fori_loop(1, shot_local, align_step, 0)
     for load in small_loads[1:]:
         load.wait()
-
-    @pl.when(jnp.logical_not(has_left))
-    def _():
-        for s in range(shot_local):
-            ext[s * ext_rows : s * ext_rows + halo_rows, :] = jnp.zeros((halo_rows, LANES), jnp.float32)
-
-    @pl.when(jnp.logical_not(has_right))
-    def _():
-        for s in range(shot_local):
-            ext[(s + 1) * ext_rows - halo_rows : (s + 1) * ext_rows, :] = jnp.zeros(
-                (halo_rows, LANES), jnp.float32
-            )
+    table_hi[...] = table[...].astype(jnp.bfloat16)
+    table_lo[...] = (table[...] - table_hi[...].astype(jnp.float32)).astype(jnp.bfloat16)
+
+    def clear(first):
+        def clear_step(unit, carry):
+            rows = pl.ds(pl.multiple_of(unit * unit_rows + first, 8), halo_rows)
+            ext[rows, :] = jnp.zeros((halo_rows, LANES), jnp.float32)
+            return carry
+
+        lax.fori_loop(0, shot_local * tiles, clear_step, 0)
+
+    pl.when(jnp.logical_not(has_left))(lambda: clear(0))
+    pl.when(jnp.logical_not(has_right))(lambda: clear(halo_rows + chan_local * 8))
+    for c in range(chan_local):
+        second[c * span : c * span + back, :] = jnp.zeros((back, LANES), jnp.float32)
 
     def forward(load, shot_id):
         values = real_dft([load(a) for a in range(outer)])
@@ -333,28 +351,33 @@
         if padded > half:
             spec[shot_id, half:padded] = jnp.zeros((padded - half, rec, 2 * LANES), jnp.float32)
         flat = spec[shot_id].reshape(padded * rec, 2 * LANES)
-        flat = split_dot(flat, fwd_hi[...], fwd_lo[...])
+        flat = split_dot(flat, table_hi[...], table_lo[...])
         spec[shot_id] = flat.reshape(padded, rec, 2 * LANES)
 
     edge_low = jnp.broadcast_to(has_left, (8, LANES))
     edge_high = jnp.broadcast_to(has_right, (8, LANES))
 
     def clean_step(s, carry):
-        to_right, to_left = halo_copies(s)
-
-        @pl.when(has_left)
-        def _():
-            to_right.wait_recv()
-
-        @pl.when(has_right)
-        def _():
-            to_left.wait_recv()
-
-        base = s * ext_rows
-
-        def median_step(tile, carry):
+        shot_id = part * shot_local + s
+        row = shifts[pl.ds(s, 1), :]
+        moves = []
+        for g in range(groups):
+            column = to_sublanes(row, rec, g * rec)
+            low = to_sublanes(lo_ref[...], rec, g * rec)
+            high = to_sublanes(hi_ref[...], rec, g * rec)
+            inside = ((low <= shot_id) & (high > shot_id)).astype(jnp.int32)
+            inside = jnp.broadcast_to(inside, (rec, LANES)) == 1
+            moves.append((whole_chunks(column, rec),) + rotate_index(column, -1, rec) + (inside,))
+
+        def unit_step(tile, carry):
+            unit = s * tiles + tile
+            to_right, to_left = halo_copies(unit)
+            pl.when(has_left)(to_right.wait_recv)
+            pl.when(has_right)(to_left.wait_recv)
+            base = unit * unit_rows
+
             def rows_at(j):
-                return ext[pl.ds(pl.multiple_of(base + j * outer + tile * 8, 8), 8), :]
+                return ext[pl.ds(pl.multiple_of(base + j * 8, 8), 8), :]
 
             rows = {j: rows_at(j) for j in range(chan_local + 2 * HALO)}
             centers = list(range(REACH, chan_local + 2 * HALO - REACH))
@@ -370,27 +393,22 @@
             centers = list(range(HALO, HALO + chan_local))
             found = median_rows(cleaned, centers)
             for j in centers:
-                start = pl.multiple_of((j - HALO) * outer + tile * 8, 8)
+                start = pl.multiple_of((j - HALO) * span + back + tile * 8, 8)
                 second[pl.ds(start, 8), :] = cleaned[j] - found[j]
+
+            for g in range(groups):
+                chosen, index, crossed, inside = moves[g]
+                chunks = [
+                    second[pl.ds(g * rec * span + tile * 8 + a, rec, stride=span), :]
+                    for a in range(back + 8)
+                ]
+                for a, value in enumerate(move_later(chunks, chosen, index, crossed)):
+                    up[s, g, tile * 8 + a] = jnp.where(inside, value, 0.0)
+            for offset in range(1, groups):
+                part_copy(s, tile, offset).start()
             return carry
 
-        lax.fori_loop(0, outer // 8, median_step, 0)
-
-        shot_id = part * shot_local + s
-        row = shifts[pl.ds(s, 1), :]
-        for g in range(groups):
-            column = to_sublanes(row, rec, g * rec)
-            low = to_sublanes(lo_ref[...], rec, g * rec)
-            high = to_sublanes(hi_ref[...], rec, g * rec)
-            inside = jnp.broadcast_to(((low <= shot_id) & (high > shot_id)).astype(jnp.int32), (rec, LANES)) == 1
-            chunks = [
-                second[pl.ds(g * rec * outer + a, rec, stride=outer), :] for a in range(outer)
-            ]
-            moved = move(chunks, column, -1, rec)
-            for a in range(outer):
-                up[s, g, a] = jnp.where(inside, moved[a], 0.0)
-        for offset in range(1, groups):
-            part_copy(s, offset).start()
+        lax.fori_loop(0, tiles, unit_step, 0)
         forward(lambda a: up[s, part, a], shot_id)
 
         @pl.when(s > 0)
@@ -401,7 +419,8 @@
 
     def arrive(s):
         for offset in range(1, groups):
-            part_copy(s, offset).wait_recv()
+            for tile in range(tiles):
+                part_copy(s, tile, offset).wait_recv()
             source = lax.rem(part + groups - offset, groups)
             shot_id = source * shot_local + s
             forward(lambda a: got[shot_id, a], shot_id)
@@ -426,7 +445,7 @@
         values = complex_dft(kept, 1)
         for s in range(shots):
             spec[s, c, :, 0:LANES] = values[s][0]
-            spec[s, c, :, LANES : 2 * LANES] = values[s][1]
+            spec[s, c, :, LANES : 2 * LANES] = -values[s][1]
         return carry
 
     lax.fori_loop(0, half, dip_step, 0)
@@ -435,42 +454,36 @@
     batch = shots // 2
     for first in range(0, shots, batch):
         flat = spec[first : first + batch].reshape(batch * padded * rec, 2 * LANES)
-        flat = split_dot(flat, inv_hi[...], inv_lo[...])
+        flat = split_dot(flat, table_hi[...], table_lo[...])
         spec[first : first + batch] = flat.reshape(batch, padded, rec, 2 * LANES)
+
+    def out_copy(s):
+        return pltpu.make_async_copy(out.at[s], out_hbm.at[s], out_sem.at[s])
 
     def back_step(s, carry):
         values = []
         for c in range(half):
-            re, im = spec[s, c, :, 0:LANES], spec[s, c, :, LANES : 2 * LANES]
-            cos, sin = twist[0, c : c + 1, :], twist[1, c : c + 1, :]
-            values.append((re * cos - im * sin, im * cos + re * sin))
+            re, minus = spec[s, c, :, 0:LANES], spec[s, c, :, LANES : 2 * LANES]
+            cos, sin = twist[2, c : c + 1, :], twist[3, c : c + 1, :]
+            values.append((re * cos + minus * sin, re * sin - minus * cos))
         for a, value in enumerate(real_inverse(values, outer)):
             out[s, :, a * LANES : (a + 1) * LANES] = value
+        out_copy(s).start()
         return carry
 
     lax.fori_loop(0, shots, back_step, 0)
 
-    def drain_step(s, carry):
-        to_right, to_left = halo_copies(s)
-
-        @pl.when(has_right)
-        def _():
-            to_right.wait_send()
-
-        @pl.when(has_left)
-        def _():
-            to_left.wait_send()
-
+    def drain_step(unit, carry):
+        to_right, to_left = halo_copies(unit)
+        pl.when(has_right)(to_right.wait_send)
+        pl.when(has_left)(to_left.wait_send)
         for offset in range(1, groups):
-            part_copy(s, offset).wait_send()
+            part_copy(unit // tiles, unit % tiles, offset).wait_send()
         return carry
 
-    lax.fori_loop(0, shot_local, drain_step, 0)
-
-
-def halves(table):
-    high = table.astype(jnp.bfloat16)
-    return high, (table - high.astype(np.float64)).astype(jnp.bfloat16)
+    lax.fori_loop(0, shot_local * tiles, drain_step, 0)
+    for s in range(shots):
+        out_copy(s).wait()
 
 
 def tables(shots, length):
@@ -478,12 +491,11 @@
     ids = np.arange(LANES)
     angles = 2.0 * np.pi * (np.outer(ids, ids) % LANES) / LANES
     cos, sin = np.cos(angles), np.sin(angles)
-    forward = np.block([[cos, -sin], [sin, cos]])
-    inverse = np.block([[cos, sin], [-sin, cos]]) / (shots * length)
+    table = np.block([[cos, -sin], [sin, cos]]).astype(np.float32)
     product = np.outer(np.arange(outer // 2 + 1), ids) % length
     angles = 2.0 * np.pi * product / length
-    twist = np.stack([np.cos(angles), np.sin(angles)]).astype(np.float32)
-    return halves(forward) + halves(inverse) + (twist,)
+    twist = np.stack([np.cos(angles), np.sin(angles)])
+    return table, np.concatenate([twist / (shots * length), twist]).astype(np.float32)
 
 
 def local(groups, blocks, traces, shifts, aperture_lo, aperture_hi, dip_band):
@@ -492,31 +504,36 @@
     rec = chan_local // groups
     shots = groups * shot_local
     padded = outer // 2 + 2
-    constants = [jnp.asarray(table) for table in tables(shots, length)]
+    constants = [jnp.asarray(item) for item in tables(shots, length)]
     operands = [
         traces, shifts, aperture_lo[None, :], aperture_hi[None, :], dip_band[None, :], *constants
     ]
     others = max(groups - 1, 1)
+    units = shot_local * (outer // 8)
     return pl.pallas_call(
         functools.partial(kernel, groups, blocks),
         out_shape=jax.ShapeDtypeStruct((shots, rec, length), jnp.float32),
         in_specs=[pl.BlockSpec(memory_space=pltpu.HBM)] * len(operands),
-        out_specs=pl.BlockSpec(memory_space=pltpu.VMEM),
+        out_specs=pl.BlockSpec(memory_space=pltpu.HBM),
         scratch_shapes=[pltpu.VMEM(item.shape, item.dtype) for item in operands] + [
             pltpu.VMEM((shot_local * (chan_local + 2 * HALO) * outer, LANES), jnp.float32),
-            pltpu.VMEM((chan_local * outer, LANES), jnp.float32),
+            pltpu.VMEM((chan_local * (outer + outer // 4), LANES), jnp.float32),
             pltpu.VMEM((shot_local, groups, outer, rec, LANES), jnp.float32),
             pltpu.VMEM((shots, outer, rec, LANES), jnp.float32),
             pltpu.VMEM((shots, padded, rec, 2 * LANES), jnp.float32),
-            pltpu.SemaphoreType.DMA((shot_local, 2)),
-            pltpu.SemaphoreType.DMA((shot_local, 2)),
-            pltpu.SemaphoreType.DMA((shot_local, others)),
-            pltpu.SemaphoreType.DMA((shot_local, others)),
+            pltpu.VMEM((shots, rec, length), jnp.float32),
+            pltpu.VMEM((2 * LANES, 2 * LANES), jnp.bfloat16),
+            pltpu.VMEM((2 * LANES, 2 * LANES), jnp.bfloat16),
+            pltpu.SemaphoreType.DMA((units, 2)),
+            pltpu.SemaphoreType.DMA((units, 2)),
+            pltpu.SemaphoreType.DMA((units, others)),
+            pltpu.SemaphoreType.DMA((units, others)),
             pltpu.SemaphoreType.DMA((shot_local,)),
             pltpu.SemaphoreType.DMA((len(operands) - 1,)),
+            pltpu.SemaphoreType.DMA((shots,)),
         ],
         compiler_params=pltpu.CompilerParams(
-            collective_id=0, has_side_effects=True, vmem_limit_bytes=48 * 1024 * 1024
+            collective_id=0, has_side_effects=True, vmem_limit_bytes=60 * 1024 * 1024
         ),
     )(*operands)
 

time: 34.4 us -> 27.6 us (0.80)
  local copies, waits for them, and re-layouts: 7.24 us -> 2.27 us
  Pallas kernels: 26.8 us -> 25.2 us
    unnamed x21 -> x1, local copies, waits for them, and re-layouts: 7.24 us -> 2.27 us
    pallas_call x1, Pallas kernels: 26.8 us -> 25.2 us  [local(): pl.pallas_call(functools.partial(kernel, groups, blocks), out_shape=jax.S...]
where the time goes in v2:
time: 27.6 us; the launch traced here: 27.4 us
  Pallas kernels  25.2 us (91%)
  local copies, waits for them, and re-layouts  2.27 us (8%)
    pallas_call x1, Pallas kernels, local(): pl.pallas_call(functools.partial(kernel, groups, blocks), out_shape=jax.S...  25.2 us
    unnamed x1, local copies, waits for them, and re-layouts  2.27 us

profile of v2, /device:TPU:9, one launch (start us, length us, event | category | flops | bytes accessed | tf_op | source)
XLA Modules:
  0.0 27.4 jit_solution(3920323749974066398)
XLA Ops:
  0.0 25.2 %shard_map.73 = f32[8,8,4096]{2,1,0:T(8,128)} custom-call(f32[4,16,4096]{2,1,0:T(8,128)} %traces_hbm.1, s32[4,16]{1,0:T(4,128)} %rest_0_.1, s32[1,16]{1,0:T(1,128)} %bitcast.3, s32[1,16]{1,0:T(1,128)} %bitcast.4, s32[1,16]{1,0:T(1,128)} %bitcast.5, f32[256,256]{1,0:T(8,128)} %constant.4.clone.rest_4_, f32[4,17,128]{2,1,0:T(8,128)} %constant.5.clone.rest_5_), custom_call_target="tpu_custom_call" | custom-call | tf_op jit(solution)/shard_map/pallas_call | solution.py:513
  25.2 2.3 %copy.9 = f32[8,8,4096]{2,1,0:T(8,128)} copy(f32[8,8,4096]{2,1,0:T(8,128)} %shard_map.73) | data formatting | bytes 2097152

commit v3 on v2

--- a/solution.py
+++ b/solution.py
@@ -357,6 +357,11 @@
     edge_low = jnp.broadcast_to(has_left, (8, LANES))
     edge_high = jnp.broadcast_to(has_right, (8, LANES))
 
+    def drain_parts(s):
+        for tile in range(tiles):
+            for offset in range(1, groups):
+                part_copy(s, tile, offset).wait_send()
+
     def clean_step(s, carry):
         shot_id = part * shot_local + s
         row = shifts[pl.ds(s, 1), :]
@@ -426,12 +431,22 @@
             forward(lambda a: got[shot_id, a], shot_id)
 
     lax.fori_loop(0, shot_local, clean_step, 0)
+
+    def drain_step(unit, carry):
+        to_right, to_left = halo_copies(unit)
+        pl.when(has_right)(to_right.wait_send)
+        pl.when(has_left)(to_left.wait_send)
+        return carry
+
+    lax.fori_loop(0, shot_local * tiles, drain_step, 0)
+    for s in range(shot_local - 1):
+        drain_parts(s)
     arrive(shot_local - 1)
 
     band = jnp.broadcast_to(to_sublanes(band_ref[...], rec, part * rec), (rec, LANES))
     lane_ids = lax.broadcasted_iota(jnp.int32, (rec, LANES), 1)
 
-    def dip_step(c, carry):
+    for c in range(half):
         frequency = lane_ids * outer + c
         freq_abs = jnp.minimum(frequency, length - frequency)
         values = [
@@ -446,9 +461,6 @@
         for s in range(shots):
             spec[s, c, :, 0:LANES] = values[s][0]
             spec[s, c, :, LANES : 2 * LANES] = -values[s][1]
-        return carry
-
-    lax.fori_loop(0, half, dip_step, 0)
 
     padded = spec.shape[1]
     batch = shots // 2
@@ -460,33 +472,29 @@
     def out_copy(s):
         return pltpu.make_async_copy(out.at[s], out_hbm.at[s], out_sem.at[s])
 
-    def back_step(s, carry):
+    def back(s):
         values = []
         for c in range(half):
             re, minus = spec[s, c, :, 0:LANES], spec[s, c, :, LANES : 2 * LANES]
-            cos, sin = twist[2, c : c + 1, :], twist[3, c : c + 1, :]
+            cos, sin = twist[0, c : c + 1, :], twist[1, c : c + 1, :]
             values.append((re * cos + minus * sin, re * sin - minus * cos))
         for a, value in enumerate(real_inverse(values, outer)):
             out[s, :, a * LANES : (a + 1) * LANES] = value
         out_copy(s).start()
+
+    def back_step(pair, carry):
+        back(2 * pair)
+        back(2 * pair + 1)
         return carry
 
-    lax.fori_loop(0, shots, back_step, 0)
-
-    def drain_step(unit, carry):
-        to_right, to_left = halo_copies(unit)
-        pl.when(has_right)(to_right.wait_send)
-        pl.when(has_left)(to_left.wait_send)
-        for offset in range(1, groups):
-            part_copy(unit // tiles, unit % tiles, offset).wait_send()
-        return carry
-
-    lax.fori_loop(0, shot_local * tiles, drain_step, 0)
+    lax.fori_loop(0, shots // 2, back_step, 0)
+
+    drain_parts(shot_local - 1)
     for s in range(shots):
         out_copy(s).wait()
 
 
-def tables(shots, length):
+def tables(length):
     outer = length // LANES
     ids = np.arange(LANES)
     angles = 2.0 * np.pi * (np.outer(ids, ids) % LANES) / LANES
@@ -495,7 +503,7 @@
     product = np.outer(np.arange(outer // 2 + 1), ids) % length
     angles = 2.0 * np.pi * product / length
     twist = np.stack([np.cos(angles), np.sin(angles)])
-    return table, np.concatenate([twist / (shots * length), twist]).astype(np.float32)
+    return table, twist.astype(np.float32)
 
 
 def local(groups, blocks, traces, shifts, aperture_lo, aperture_hi, dip_band):
@@ -504,13 +512,13 @@
     rec = chan_local // groups
     shots = groups * shot_local
     padded = outer // 2 + 2
-    constants = [jnp.asarray(item) for item in tables(shots, length)]
+    constants = [jnp.asarray(item) for item in tables(length)]
     operands = [
         traces, shifts, aperture_lo[None, :], aperture_hi[None, :], dip_band[None, :], *constants
     ]
     others = max(groups - 1, 1)
     units = shot_local * (outer // 8)
-    return pl.pallas_call(
+    summed = pl.pallas_call(
         functools.partial(kernel, groups, blocks),
         out_shape=jax.ShapeDtypeStruct((shots, rec, length), jnp.float32),
         in_specs=[pl.BlockSpec(memory_space=pltpu.HBM)] * len(operands),
@@ -536,6 +544,7 @@
             collective_id=0, has_side_effects=True, vmem_limit_bytes=60 * 1024 * 1024
         ),
     )(*operands)
+    return summed * np.float32(1.0 / (shots * length))
 
 
 def solution(mesh):

time: 27.6 us -> 27.4 us (level)
  other arithmetic: 0 us -> 2.27 us
  local copies, waits for them, and re-layouts: 2.27 us -> 0 us
    mul x0 -> x1, other arithmetic: none -> 2.27 us  [local(): return summed * np.float32(1.0 / (shots * length))]
    unnamed x1 -> x0, local copies, waits for them, and re-layouts: 2.27 us -> none
where the time goes in v3:
time: 27.4 us; the launch traced here: 27.3 us
  Pallas kernels  25 us (91%)
  other arithmetic  2.27 us (8%)
    pallas_call x1, Pallas kernels, local(): pl.pallas_call(functools.partial(kernel, groups, blocks), out_shape=jax.S...  25 us
    mul x1, other arithmetic, local(): return summed * np.float32(1.0 / (shots * length))  2.27 us

profile of v3, /device:TPU:9, one launch (start us, length us, event | category | flops | bytes accessed | tf_op | source)
XLA Modules:
  0.0 27.3 jit_solution(9765983872467649235)
XLA Ops:
  0.0 25.0 %shard_map.73 = f32[8,8,4096]{2,1,0:T(8,128)} custom-call(f32[4,16,4096]{2,1,0:T(8,128)} %traces_hbm.1, s32[4,16]{1,0:T(4,128)} %rest_0_.1, s32[1,16]{1,0:T(1,128)} %bitcast.3, s32[1,16]{1,0:T(1,128)} %bitcast.4, s32[1,16]{1,0:T(1,128)} %bitcast.5, f32[256,256]{1,0:T(8,128)} %constant.6.clone.rest_4_, f32[2,17,128]{2,1,0:T(8,128)} %constant.7.clone.rest_5_), custom_call_target="tpu_custom_call" | custom-call | tf_op jit(solution)/shard_map/pallas_call | solution.py:521
  25.0 2.3 %broadcast_multiply_fusion = f32[8,8,4096]{2,1,0:T(8,128)} fusion(f32[8,8,4096]{2,1,0:T(8,128)} %shard_map.73), kind=kLoop, calls=%fused_computation | loop fusion | flops 262144 | bytes 2097152 | tf_op jit(solution)/shard_map/mul | solution.py:547

commit v4 on v3

--- a/solution.py
+++ b/solution.py
@@ -174,8 +174,8 @@
     small_hbm, out_hbm, scratch = rest[:6], rest[6], rest[7:]
     traces, small, scratch = scratch[0], scratch[1:7], scratch[7:]
     shifts, lo_ref, hi_ref, band_ref, table, twist = small
-    ext, second, up, got, spec, out, table_hi, table_lo = scratch[:8]
-    halo_send, halo_recv, part_send, part_recv, load_sem, small_sem, out_sem = scratch[8:]
+    ext, second, up, got, spec, out, table_hi, table_lo, transit = scratch[:9]
+    halo_send, halo_recv, part_send, part_recv, load_sem, small_sem, out_sem, transit_send, transit_recv = scratch[9:]
     shot_local, chan_local, length = traces.shape
     outer = length // LANES
     half = outer // 2 + 1
@@ -205,7 +205,31 @@
     for load in trace_loads + small_loads[1:]:
         load.start()
 
+    planes = blocks // 4
+    relayed = groups == 2 and blocks % 4 == 0 and planes > 1 and tiles % planes == 0
+    plane, place = block // 4, block % 4
+    is_first = (place == 0).astype(jnp.int32)
+    is_last = (place == 3).astype(jnp.int32)
+    is_end = place % 3 == 0
+    left_share = is_first * plane * (tiles // planes)
+    right_share = is_last * (planes - 1 - plane) * (tiles // planes)
+    transit_share = (is_last * plane + is_first * (planes - 1 - plane)) * (tiles // planes)
+    corner = block + 3 * is_first - 3 * is_last
+    onward = jnp.minimum(jnp.maximum(block + 4 * is_first - 4 * is_last, 0), blocks - 1)
+    has_next = is_end & (block + 4 < blocks)
+    has_before = is_end & (block >= 4)
+
     barrier = pltpu.get_barrier_semaphore()
+
+    if relayed:
+        for there, other in (
+            (is_end, corner),
+            (has_next, jnp.minimum(block + 4, blocks - 1)),
+            (has_before, jnp.maximum(block - 4, 0)),
+        ):
+            @pl.when(there)
+            def _():
+                pl.semaphore_signal(barrier, inc=1, device_id=(part, other), device_id_type=mesh_id)
 
     @pl.when(has_left)
     def _():
@@ -279,6 +303,29 @@
         )
         return to_right, to_left
 
+    def corner_copy(unit, side):
+        base = pl.multiple_of(unit * unit_rows, 8)
+        start = base + chan_local * 8 if side == 0 else base + halo_rows
+        return pltpu.make_async_remote_copy(
+            src_ref=ext.at[pl.ds(start, halo_rows)],
+            dst_ref=transit.at[unit],
+            send_sem=halo_send.at[unit, side],
+            recv_sem=transit_recv.at[unit],
+            device_id=(part, corner),
+            device_id_type=mesh_id,
+        )
+
+    def onward_copy(unit):
+        start = unit * unit_rows + is_last * (halo_rows + chan_local * 8)
+        return pltpu.make_async_remote_copy(
+            src_ref=transit.at[unit],
+            dst_ref=ext.at[pl.ds(pl.multiple_of(start, 8), halo_rows)],
+            send_sem=transit_send.at[unit],
+            recv_sem=halo_recv.at[unit, is_last],
+            device_id=(part, onward),
+            device_id_type=mesh_id,
+        )
+
     def part_copy(s, tile, offset):
         other = lax.rem(part + offset, groups)
         rows = pl.ds(pl.multiple_of(tile * 8, 8), 8)
@@ -304,13 +351,22 @@
     def send_halos(s):
         for tile in range(tiles):
             to_right, to_left = halo_copies(s * tiles + tile)
-            pl.when(has_right)(to_right.start)
-            pl.when(has_left)(to_left.start)
+            if relayed:
+                pl.when(has_right & (tile >= right_share))(to_right.start)
+                pl.when(has_left & (tile >= left_share))(to_left.start)
+                pl.when(has_right & (tile < right_share))(corner_copy(s * tiles + tile, 0).start)
+                pl.when(has_left & (tile < left_share))(corner_copy(s * tiles + tile, 1).start)
+            else:
+                pl.when(has_right)(to_right.start)
+                pl.when(has_left)(to_left.start)
 
     small_loads[0].wait()
     trace_loads[0].wait()
     align(0)
     expected = has_left.astype(jnp.int32) + has_right.astype(jnp.int32) + (groups - 1)
+    if relayed:
+        for there in (is_end, has_next, has_before):
+            expected = expected + there.astype(jnp.int32)
     pl.semaphore_wait(barrier, expected)
     send_halos(0)
 
@@ -376,6 +432,13 @@
 
         def unit_step(tile, carry):
             unit = s * tiles + tile
+            if relayed:
+                @pl.when(tile < transit_share)
+                def _():
+                    moving = onward_copy(unit)
+                    corner_copy(unit, 0).wait_recv()
+                    moving.start()
+
             to_right, to_left = halo_copies(unit)
             pl.when(has_left)(to_right.wait_recv)
             pl.when(has_right)(to_left.wait_recv)
@@ -436,6 +499,8 @@
         to_right, to_left = halo_copies(unit)
         pl.when(has_right)(to_right.wait_send)
         pl.when(has_left)(to_left.wait_send)
+        if relayed:
+            pl.when(unit % tiles < transit_share)(onward_copy(unit).wait_send)
         return carry
 
     lax.fori_loop(0, shot_local * tiles, drain_step, 0)
@@ -532,6 +597,7 @@
             pltpu.VMEM((shots, rec, length), jnp.float32),
             pltpu.VMEM((2 * LANES, 2 * LANES), jnp.bfloat16),
             pltpu.VMEM((2 * LANES, 2 * LANES), jnp.bfloat16),
+            pltpu.VMEM((units, HALO * 8, LANES), jnp.float32),
             pltpu.SemaphoreType.DMA((units, 2)),
             pltpu.SemaphoreType.DMA((units, 2)),
             pltpu.SemaphoreType.DMA((units, others)),
@@ -539,6 +605,8 @@
             pltpu.SemaphoreType.DMA((shot_local,)),
             pltpu.SemaphoreType.DMA((len(operands) - 1,)),
             pltpu.SemaphoreType.DMA((shots,)),
+            pltpu.SemaphoreType.DMA((units,)),
+            pltpu.SemaphoreType.DMA((units,)),
         ],
         compiler_params=pltpu.CompilerParams(
             collective_id=0, has_side_effects=True, vmem_limit_bytes=60 * 1024 * 1024

time: 27.4 us -> 30.7 us (1.12)
  the two profiles are of different devices: /device:TPU:9 before, /device:TPU:26 now
where the time goes in v4:
time: 30.7 us; the launch traced here: 30.5 us
  Pallas kernels  28.2 us (92%)
  other arithmetic  2.27 us (7%)
    pallas_call x1, Pallas kernels, local(): pl.pallas_call(functools.partial(kernel, groups, blocks), out_shape=jax.S...  28.2 us
    mul x1, other arithmetic, local(): return summed * np.float32(1.0 / (shots * length))  2.27 us

profile of v4, /device:TPU:26, one launch (start us, length us, event | category | flops | bytes accessed | tf_op | source)
XLA Modules:
  0.0 30.5 jit_solution(10994857922818679095)
XLA Ops:
  0.0 28.2 %shard_map.73 = f32[8,8,4096]{2,1,0:T(8,128)} custom-call(f32[4,16,4096]{2,1,0:T(8,128)} %traces_hbm.1, s32[4,16]{1,0:T(4,128)} %rest_0_.1, s32[1,16]{1,0:T(1,128)} %bitcast.3, s32[1,16]{1,0:T(1,128)} %bitcast.4, s32[1,16]{1,0:T(1,128)} %bitcast.5, f32[256,256]{1,0:T(8,128)} %constant.6.clone.rest_4_, f32[2,17,128]{2,1,0:T(8,128)} %constant.7.clone.rest_5_), custom_call_target="tpu_custom_call" | custom-call | tf_op jit(solution)/shard_map/pallas_call | solution.py:586
  28.2 2.3 %broadcast_multiply_fusion = f32[8,8,4096]{2,1,0:T(8,128)} fusion(f32[8,8,4096]{2,1,0:T(8,128)} %shard_map.73), kind=kLoop, calls=%fused_computation | loop fusion | flops 262144 | bytes 2097152 | tf_op jit(solution)/shard_map/mul | solution.py:615

commit v5 on v3

--- a/solution.py
+++ b/solution.py
@@ -171,11 +171,14 @@
     groups, blocks,
     traces_hbm, *rest,
 ):
-    small_hbm, out_hbm, scratch = rest[:6], rest[6], rest[7:]
-    traces, small, scratch = scratch[0], scratch[1:7], scratch[7:]
-    shifts, lo_ref, hi_ref, band_ref, table, twist = small
-    ext, second, up, got, spec, out, table_hi, table_lo = scratch[:8]
-    halo_send, halo_recv, part_send, part_recv, load_sem, small_sem, out_sem = scratch[8:]
+    numbers_hbm, rows_hbm, out, scratch = rest[0], rest[1], rest[2], rest[3:]
+    traces, small, scratch = scratch[0], scratch[1:4], scratch[4:]
+    numbers, table, twist = small
+    small_hbm = (
+        numbers_hbm, rows_hbm.at[0 : 2 * LANES], rows_hbm.at[2 * LANES : 2 * LANES + twist.shape[0]],
+    )
+    ext, second, up, got, spec, table_hi, table_lo = scratch[:7]
+    halo_send, halo_recv, part_send, part_recv, load_sem, small_sem = scratch[7:]
     shot_local, chan_local, length = traces.shape
     outer = length // LANES
     half = outer // 2 + 1
@@ -292,7 +295,7 @@
         )
 
     def align(s):
-        row = shifts[pl.ds(s, 1), :]
+        row = numbers[pl.ds(s, 1), :]
         for top in range(0, chan_local, 8):
             column = to_sublanes(row, 8, top)
             chunks = [traces[s, top : top + 8, a * LANES : (a + 1) * LANES] for a in range(outer)]
@@ -344,7 +347,7 @@
         values = real_dft([load(a) for a in range(outer)])
         for c in range(half):
             re, im = values[c]
-            cos, sin = twist[0, c : c + 1, :], twist[1, c : c + 1, :]
+            cos, sin = twist[c : c + 1, 0:LANES], twist[c : c + 1, LANES : 2 * LANES]
             spec[shot_id, c, :, 0:LANES] = re * cos + im * sin
             spec[shot_id, c, :, LANES : 2 * LANES] = im * cos - re * sin
         padded = spec.shape[1]
@@ -364,12 +367,12 @@
 
     def clean_step(s, carry):
         shot_id = part * shot_local + s
-        row = shifts[pl.ds(s, 1), :]
+        row = numbers[pl.ds(s, 1), :]
         moves = []
         for g in range(groups):
             column = to_sublanes(row, rec, g * rec)
-            low = to_sublanes(lo_ref[...], rec, g * rec)
-            high = to_sublanes(hi_ref[...], rec, g * rec)
+            low = to_sublanes(numbers[shot_local : shot_local + 1, :], rec, g * rec)
+            high = to_sublanes(numbers[shot_local + 1 : shot_local + 2, :], rec, g * rec)
             inside = ((low <= shot_id) & (high > shot_id)).astype(jnp.int32)
             inside = jnp.broadcast_to(inside, (rec, LANES)) == 1
             moves.append((whole_chunks(column, rec),) + rotate_index(column, -1, rec) + (inside,))
@@ -443,7 +446,7 @@
         drain_parts(s)
     arrive(shot_local - 1)
 
-    band = jnp.broadcast_to(to_sublanes(band_ref[...], rec, part * rec), (rec, LANES))
+    band = jnp.broadcast_to(to_sublanes(numbers[shot_local + 2 : shot_local + 3, :], rec, part * rec), (rec, LANES))
     lane_ids = lax.broadcasted_iota(jnp.int32, (rec, LANES), 1)
 
     for c in range(half):
@@ -469,18 +472,14 @@
         flat = split_dot(flat, table_hi[...], table_lo[...])
         spec[first : first + batch] = flat.reshape(batch, padded, rec, 2 * LANES)
 
-    def out_copy(s):
-        return pltpu.make_async_copy(out.at[s], out_hbm.at[s], out_sem.at[s])
-
     def back(s):
         values = []
         for c in range(half):
             re, minus = spec[s, c, :, 0:LANES], spec[s, c, :, LANES : 2 * LANES]
-            cos, sin = twist[0, c : c + 1, :], twist[1, c : c + 1, :]
+            cos, sin = twist[c : c + 1, 0:LANES], twist[c : c + 1, LANES : 2 * LANES]
             values.append((re * cos + minus * sin, re * sin - minus * cos))
         for a, value in enumerate(real_inverse(values, outer)):
             out[s, :, a * LANES : (a + 1) * LANES] = value
-        out_copy(s).start()
 
     def back_step(pair, carry):
         back(2 * pair)
@@ -490,8 +489,6 @@
     lax.fori_loop(0, shots // 2, back_step, 0)
 
     drain_parts(shot_local - 1)
-    for s in range(shots):
-        out_copy(s).wait()
 
 
 def tables(length):
@@ -500,10 +497,12 @@
     angles = 2.0 * np.pi * (np.outer(ids, ids) % LANES) / LANES
     cos, sin = np.cos(angles), np.sin(angles)
     table = np.block([[cos, -sin], [sin, cos]]).astype(np.float32)
-    product = np.outer(np.arange(outer // 2 + 1), ids) % length
-    angles = 2.0 * np.pi * product / length
-    twist = np.stack([np.cos(angles), np.sin(angles)])
-    return table, twist.astype(np.float32)
+    half = outer // 2 + 1
+    angles = 2.0 * np.pi * (np.outer(np.arange(half), ids) % length) / length
+    rows = np.zeros((16 * 2 * LANES, 2 * LANES), np.float32)
+    rows[: 2 * LANES] = table
+    rows[2 * LANES : 2 * LANES + half] = np.concatenate([np.cos(angles), np.sin(angles)], axis=1)
+    return rows
 
 
 def local(groups, blocks, traces, shifts, aperture_lo, aperture_hi, dip_band):
@@ -512,24 +511,27 @@
     rec = chan_local // groups
     shots = groups * shot_local
     padded = outer // 2 + 2
-    constants = [jnp.asarray(item) for item in tables(length)]
-    operands = [
-        traces, shifts, aperture_lo[None, :], aperture_hi[None, :], dip_band[None, :], *constants
-    ]
+    constants = jnp.asarray(tables(length))
+    twist_rows = -(-(outer // 2 + 1) // 8) * 8
+    numbers = jnp.concatenate(
+        [shifts, aperture_lo[None, :], aperture_hi[None, :], dip_band[None, :]], axis=0
+    )
+    operands = [traces, numbers, constants]
     others = max(groups - 1, 1)
     units = shot_local * (outer // 8)
     summed = pl.pallas_call(
         functools.partial(kernel, groups, blocks),
         out_shape=jax.ShapeDtypeStruct((shots, rec, length), jnp.float32),
         in_specs=[pl.BlockSpec(memory_space=pltpu.HBM)] * len(operands),
-        out_specs=pl.BlockSpec(memory_space=pltpu.HBM),
-        scratch_shapes=[pltpu.VMEM(item.shape, item.dtype) for item in operands] + [
+        out_specs=pl.BlockSpec(memory_space=pltpu.VMEM),
+        scratch_shapes=[pltpu.VMEM(item.shape, item.dtype) for item in operands[:-1]] + [
+            pltpu.VMEM((2 * LANES, 2 * LANES), jnp.float32),
+            pltpu.VMEM((twist_rows, 2 * LANES), jnp.float32),
             pltpu.VMEM((shot_local * (chan_local + 2 * HALO) * outer, LANES), jnp.float32),
             pltpu.VMEM((chan_local * (outer + outer // 4), LANES), jnp.float32),
             pltpu.VMEM((shot_local, groups, outer, rec, LANES), jnp.float32),
             pltpu.VMEM((shots, outer, rec, LANES), jnp.float32),
             pltpu.VMEM((shots, padded, rec, 2 * LANES), jnp.float32),
-            pltpu.VMEM((shots, rec, length), jnp.float32),
             pltpu.VMEM((2 * LANES, 2 * LANES), jnp.bfloat16),
             pltpu.VMEM((2 * LANES, 2 * LANES), jnp.bfloat16),
             pltpu.SemaphoreType.DMA((units, 2)),
@@ -537,11 +539,10 @@
             pltpu.SemaphoreType.DMA((units, others)),
             pltpu.SemaphoreType.DMA((units, others)),
             pltpu.SemaphoreType.DMA((shot_local,)),
-            pltpu.SemaphoreType.DMA((len(operands) - 1,)),
-            pltpu.SemaphoreType.DMA((shots,)),
+            pltpu.SemaphoreType.DMA((len(operands),)),
         ],
         compiler_params=pltpu.CompilerParams(
-            collective_id=0, has_side_effects=True, vmem_limit_bytes=60 * 1024 * 1024
+            collective_id=0, has_side_effects=True, vmem_limit_bytes=52 * 1024 * 1024
         ),
     )(*operands)
     return summed * np.float32(1.0 / (shots * length))

time: 27.4 us -> 26.2 us (0.956)
  Pallas kernels: 25 us -> 24.3 us
  other arithmetic: 2.27 us -> 1.8 us
    mul x1, other arithmetic: 2.27 us -> 1.06 us  [local(): return summed * np.float32(1.0 / (shots * length))]
    concatenate x0 -> x1, other arithmetic: none -> 0.74 us  [local(): jnp.concatenate([shifts, aperture_lo[None, :], aperture_hi[None, :], dip_...]
    pallas_call x1, Pallas kernels: 25 us -> 24.3 us  [local(): pl.pallas_call(functools.partial(kernel, groups, blocks), out_shape=jax.S...]
where the time goes in v5:
time: 26.2 us; the launch traced here: 26.1 us
  Pallas kernels  24.3 us (93%)
  other arithmetic  1.8 us (7%)
    pallas_call x1, Pallas kernels, local(): pl.pallas_call(functools.partial(kernel, groups, blocks), out_shape=jax.S...  24.3 us
    mul x1, other arithmetic, local(): return summed * np.float32(1.0 / (shots * length))  1.06 us
    concatenate x1, other arithmetic, local(): jnp.concatenate([shifts, aperture_lo[None, :], aperture_hi[None, :], dip_...  0.74 us

profile of v5, /device:TPU:9, one launch (start us, length us, event | category | flops | bytes accessed | tf_op | source)
XLA Modules:
  0.0 26.1 jit_solution(11191298967016202355)
XLA Ops:
  0.0 0.7 %pad_add_fusion.rest_0_ = s32[7,16]{1,0:T(8,128)S(1)} fusion(s32[1,16]{1,0:T(1,128)} %bitcast.3, s32[1,16]{1,0:T(1,128)} %bitcast.4, s32[1,16]{1,0:T(1,128)} %bitcast.5, s32[4,16]{1,0:T(4,128)} %param.7), kind=kLoop, calls=%fused_computation.1 | loop fusion | flops 336 | bytes 896 | tf_op jit(solution)/shard_map/concatenate | solution.py:516
  0.7 24.3 %shard_map.64 = f32[8,8,4096]{2,1,0:T(8,128)S(1)} custom-call(f32[4,16,4096]{2,1,0:T(8,128)} %traces_hbm.1, s32[7,16]{1,0:T(8,128)S(1)} %pad_add_fusion.rest_0_, f32[4096,256]{1,0:T(8,128)} %constant.4.clone.rest_1_), custom_call_target="tpu_custom_call" | custom-call | tf_op jit(solution)/shard_map/pallas_call | solution.py:522
  25.0 1.1 %broadcast_multiply_fusion = f32[8,8,4096]{2,1,0:T(8,128)} fusion(f32[8,8,4096]{2,1,0:T(8,128)S(1)} %shard_map.64), kind=kLoop, calls=%fused_computation | loop fusion | flops 262144 | bytes 2097152 | tf_op jit(solution)/shard_map/mul | solution.py:548

commit v6 on v5

--- a/solution.py
+++ b/solution.py
@@ -305,10 +305,15 @@
                 ext[pl.ds(start, 8, stride=8), :] = moved[a]
 
     def send_halos(s):
+        odd = block % 2 == 1
         for tile in range(tiles):
             to_right, to_left = halo_copies(s * tiles + tile)
-            pl.when(has_right)(to_right.start)
-            pl.when(has_left)(to_left.start)
+            pl.when(has_right & odd)(to_right.start)
+            pl.when(has_left & jnp.logical_not(odd))(to_left.start)
+        for tile in range(tiles):
+            to_right, to_left = halo_copies(s * tiles + tile)
+            pl.when(has_right & jnp.logical_not(odd))(to_right.start)
+            pl.when(has_left & odd)(to_left.start)
 
     small_loads[0].wait()
     trace_loads[0].wait()

time: 26.2 us -> 26.2 us (level)
  no operation moved by 1% of the time
where the time goes in v6:
time: 26.2 us; the launch traced here: 26.1 us
  Pallas kernels  24.3 us (93%)
  other arithmetic  1.8 us (7%)
    pallas_call x1, Pallas kernels, local(): pl.pallas_call(functools.partial(kernel, groups, blocks), out_shape=jax.S...  24.3 us
    mul x1, other arithmetic, local(): return summed * np.float32(1.0 / (shots * length))  1.06 us
    concatenate x1, other arithmetic, local(): jnp.concatenate([shifts, aperture_lo[None, :], aperture_hi[None, :], dip_...  0.74 us

profile of v6, /device:TPU:9, one launch (start us, length us, event | category | flops | bytes accessed | tf_op | source)
XLA Modules:
  0.0 26.1 jit_solution(9996804900632551553)
XLA Ops:
  0.0 0.7 %pad_add_fusion.rest_0_ = s32[7,16]{1,0:T(8,128)S(1)} fusion(s32[1,16]{1,0:T(1,128)} %bitcast.3, s32[1,16]{1,0:T(1,128)} %bitcast.4, s32[1,16]{1,0:T(1,128)} %bitcast.5, s32[4,16]{1,0:T(4,128)} %param.7), kind=kLoop, calls=%fused_computation.1 | loop fusion | flops 336 | bytes 896 | tf_op jit(solution)/shard_map/concatenate | solution.py:521
  0.7 24.3 %shard_map.64 = f32[8,8,4096]{2,1,0:T(8,128)S(1)} custom-call(f32[4,16,4096]{2,1,0:T(8,128)} %traces_hbm.1, s32[7,16]{1,0:T(8,128)S(1)} %pad_add_fusion.rest_0_, f32[4096,256]{1,0:T(8,128)} %constant.4.clone.rest_1_), custom_call_target="tpu_custom_call" | custom-call | tf_op jit(solution)/shard_map/pallas_call | solution.py:527
  25.0 1.1 %broadcast_multiply_fusion = f32[8,8,4096]{2,1,0:T(8,128)} fusion(f32[8,8,4096]{2,1,0:T(8,128)S(1)} %shard_map.64), kind=kLoop, calls=%fused_computation | loop fusion | flops 262144 | bytes 2097152 | tf_op jit(solution)/shard_map/mul | solution.py:553
